TPU v7x, 512 devices: a whole 4x8x8 slice. The times are simulated.
512 devices in a mesh: section: 8 (over y_hi, core), dp: 64 (over x, z, y_lo).
Axes of the slice: x: 4, y: 8 (y_hi: 4, y_lo: 2; y = y_hi * 2 + y_lo), z: 8, core: 2. Of those that a mesh axis runs over, the one named last changes fastest.
Arguments:
- inputs: bfloat16 [2, 4096, 4096], P(None, 'dp'), may hold values from -6 to 6
- cotangent: bfloat16 [2, 4096, 4096], P(None, 'dp'), may hold values from -6 to 6
- doc_lengths: int32 [2, 64, 2], P(None, 'dp'), may hold values from 1 to 48, 64 in all within a row
- norm_gain: bfloat16 [8, 4096], P('section'), may hold values from 0.25 to 1.75
- w_qkv: bfloat16 [8, 4096, 192], P('section', 'dp'), may hold values from -0.09375 to 0.09375
- w_out: bfloat16 [8, 64, 4096], P('section', None, 'dp'), may hold values from -0.75 to 0.75
Outputs:
- grad_qkv: float32 [8, 4096, 192], P('section', 'dp')
- grad_out: float32 [8, 64, 4096], P('section', None, 'dp')
Inputs may be any that keep to these rules, and one draw needn't show every extreme that they name: `doc_lengths`: each row's 2 lengths add up to 64.
All inputs are finite; a program needn't handle non-finite values.
Results may differ from a plain program's by a relative error of at most 0.025.
Values may be sent and summed in bfloat16 or wider, within the bound.
A program may use at most 64 MiB of HBM per device.

v0:
```python
import jax
import jax.numpy as jnp
from jax import lax
from jax.sharding import PartitionSpec as P


def passed_along(block, axis, distance):
    devices = range(lax.axis_size(axis))
    route = [(i - distance, i) for i in devices if i - distance in devices]
    return lax.ppermute(block, axis, route)


def segments_of(lengths, count):
    ends = jnp.cumsum(lengths)
    position = jnp.arange(count, dtype=jnp.int32)
    return jnp.sum((position[:, None] >= ends[None, :]).astype(jnp.int32), axis=1)


def layer(x, gain, w_qkv, w_out, seg):
    head = w_out.shape[0]
    x_wide = x.astype(jnp.float32)
    scale = lax.rsqrt(jnp.mean(x_wide * x_wide, axis=-1, keepdims=True) + 1e-05)
    normed = (x_wide * scale * gain.astype(jnp.float32)).astype(jnp.bfloat16)
    qkv = jnp.dot(normed, w_qkv, preferred_element_type=jnp.float32).astype(jnp.bfloat16)
    query = qkv[:, :head]
    keys = qkv[:, head : 2 * head]
    values = qkv[:, 2 * head :]
    scores = jnp.dot(query, keys.T, preferred_element_type=jnp.float32) * head ** (-0.5)
    rows = jnp.arange(x.shape[0], dtype=jnp.int32)
    allowed = (seg[:, None] == seg[None, :]) & (rows[:, None] >= rows[None, :])
    scores = jnp.where(allowed, scores, -1e30)
    probs = jax.nn.softmax(scores, axis=-1).astype(jnp.bfloat16)
    attended = jnp.dot(probs, values, preferred_element_type=jnp.float32).astype(jnp.bfloat16)
    return (x_wide + jnp.dot(attended, w_out, preferred_element_type=jnp.float32)).astype(
        jnp.bfloat16
    )


def body(inputs, cotangent, doc_lengths, norm_gain, w_qkv, w_out):
    sections = lax.axis_size("section")
    section = lax.axis_index("section")
    micro = inputs.shape[0]
    count = inputs.shape[1]
    segs = jax.vmap(lambda lens: segments_of(lens, count))(doc_lengths[:, 0, :])
    gain = norm_gain[0]
    full_qkv, full_out = (
        lax.all_gather(w_qkv[0], "dp", axis=0, tiled=True),
        lax.all_gather(w_out[0], "dp", axis=1, tiled=True),
    )
    total_steps = micro + sections - 1
    empty = jnp.zeros(inputs.shape[1:], inputs.dtype)

    def forward_at(step, incoming, saved):
        index = step - section
        live = (index >= 0) & (index < micro)
        slot = jnp.clip(index, 0, micro - 1)
        first = lax.dynamic_index_in_dim(inputs, slot, 0, keepdims=False)
        x = jnp.where(section == 0, first, incoming)
        seg = lax.dynamic_index_in_dim(segs, slot, 0, keepdims=False)
        out = layer(x, gain, full_qkv, full_out, seg)
        old = lax.dynamic_index_in_dim(saved, slot, 0, keepdims=False)
        saved = lax.dynamic_update_index_in_dim(saved, jnp.where(live, x, old), slot, 0)
        return (out, saved)

    def forward_step(carry, step):
        incoming, saved = carry
        out, saved = forward_at(step, incoming, saved)
        incoming = passed_along(out, "section", 1)
        return ((incoming, saved), None)

    start_saved = jnp.zeros(inputs.shape, inputs.dtype)
    (incoming, saved), _ = lax.scan(
        forward_step, (empty, start_saved), jnp.arange(total_steps - 1, dtype=jnp.int32)
    )
    _, saved = forward_at(jnp.int32(total_steps - 1), incoming, saved)
    back_qkv, back_out = (
        lax.all_gather(w_qkv[0], "dp", axis=0, tiled=True),
        lax.all_gather(w_out[0], "dp", axis=1, tiled=True),
    )

    def backward_at(step, incoming, sum_qkv, sum_out):
        index = step - (sections - 1 - section)
        live = (index >= 0) & (index < micro)
        slot = jnp.clip(index, 0, micro - 1)
        last = lax.dynamic_index_in_dim(cotangent, slot, 0, keepdims=False)
        grad_y = jnp.where(section == sections - 1, last, incoming)
        x = lax.dynamic_index_in_dim(saved, slot, 0, keepdims=False)
        seg = lax.dynamic_index_in_dim(segs, slot, 0, keepdims=False)
        _, pull = jax.vjp(lambda a, b, c: layer(a, gain, b, c, seg), x, back_qkv, back_out)
        grad_x, grad_q, grad_o = pull(grad_y)
        sum_qkv = sum_qkv + jnp.where(live, grad_q.astype(jnp.float32), 0.0)
        sum_out = sum_out + jnp.where(live, grad_o.astype(jnp.float32), 0.0)
        return (grad_x, sum_qkv, sum_out)

    def backward_step(carry, step):
        incoming, sum_qkv, sum_out = carry
        grad_x, sum_qkv, sum_out = backward_at(step, incoming, sum_qkv, sum_out)
        incoming = passed_along(grad_x, "section", -1)
        return ((incoming, sum_qkv, sum_out), None)

    zero_qkv = jnp.zeros(back_qkv.shape, jnp.float32)
    zero_out = jnp.zeros(back_out.shape, jnp.float32)
    (incoming, sum_qkv, sum_out), _ = lax.scan(
        backward_step, (empty, zero_qkv, zero_out), jnp.arange(total_steps - 1, dtype=jnp.int32)
    )
    _, sum_qkv, sum_out = backward_at(jnp.int32(total_steps - 1), incoming, sum_qkv, sum_out)
    share_qkv, share_out = (
        lax.psum_scatter(sum_qkv, "dp", scatter_dimension=0, tiled=True),
        lax.psum_scatter(sum_out, "dp", scatter_dimension=1, tiled=True),
    )
    return (share_qkv[None], share_out[None])


def solution(mesh):
    return jax.shard_map(
        body,
        mesh=mesh,
        in_specs=(
            P(None, "dp", None),
            P(None, "dp", None),
            P(None, "dp", None),
            P("section", None),
            P("section", "dp", None),
            P("section", None, "dp"),
        ),
        out_specs=(P("section", "dp", None), P("section", None, "dp")),
        check_vma=False,
    )
```

profile of v0, /device:TPU:16, one launch (start us, length us, event | category | flops | bytes accessed | tf_op | source)
XLA Modules:
  0.0 1309.9 jit_solution(11713632534645186579)
XLA Ops:
  9.7 185.1 %all-gather.1 = bf16[1,64,4096]{1,0,2:T(2,128)(2,1)S(1)} all-gather(bf16[1,64,64]{1,0,2:T(2,128)(2,1)S(1)} %copy.16), channel_id=3, replica_groups=mesh['section'=8,'dp'=64] {'dp'}, dimensions={2}, use_global_device_ids=true | all-gather | bytes 532480 | tf_op jit(solution)/shard_map/all_gather | solution.py:48
  194.7 3.6 copy.17
  198.5 120.8 %all-gather.4.cloned.1.call-done = bf16[1,4096,192]{2,1,0:T(8,128)(2,1)} async-done(((bf16[1,64,192]{2,1,0:T(8,128)(2,1)}), bf16[1,4096,192]{2,1,0:T(8,128)(2,1)}) %all-gather.4.cloned.1.call-update) | async-done | bytes 1572880 | tf_op jit(solution)/shard_map/all_gather | solution.py:47
  320.3 157.4 %while.30 = (s32[]{:T(128)}, bf16[64,4096]{1,0:T(8,128)(2,1)}, bf16[2,64,4096]{2,1,0:T(8,128)(2,1)S(1)}, pred[]{:T(512)}, s32[8]{0:T(128)S(1)}, /*index=5*/s32[]...) while((s32[]{:T(128)}, bf16[64,4096]{1,0:T(8,128)(2,1)}, ...), condition=%wide.region_6.7_spmd, body=%wide.region_2.6_spmd.sunk | while | flops 138477504 | bytes 20632148 | solution.py:72
  326.7 1.9 collective-permute-start
  328.6 9.6 collective-permute-done
  345.4 1.9 collective-permute-start
  347.3 9.6 collective-permute-done
  364.1 12.1 collective-permute-start
  384.8 11.2 collective-permute-start
  404.7 11.1 collective-permute-start
  424.6 11.1 collective-permute-start
  444.4 11.1 collective-permute-start
  464.2 11.2 collective-permute-start
  481.1 157.0 %while.31 = (s32[]{:T(128)}, bf16[64,4096]{1,0:T(8,128)(2,1)}, f32[4096,192]{0,1:T(8,128)}, f32[64,4096]{1,0:T(8,128)}, pred[]{:T(512)}, /*index=5*/s32[8]{0:T(1...) while((s32[]{:T(128)}, bf16[64,4096]{1,0:T(8,128)(2,1)}, ...), condition=%wide.region_13.14_spmd.clone, body=%wide.region_7.13_spmd.clone.sunk | while | flops 384602496 | bytes 32000636 | solution.py:103
  487.8 1.9 collective-permute-start.1
  489.7 2.6 fusion.168
  492.2 2.4 fusion.167
  494.6 6.0 collective-permute-done.1
  507.3 1.9 collective-permute-start.1
  509.2 2.9 fusion.168
  512.1 4.3 fusion.167
  516.4 4.6 collective-permute-done.1
  527.6 1.9 collective-permute-start.1
  529.5 2.9 fusion.168
  532.4 4.3 fusion.167
  536.6 3.8 collective-permute-done.1
  549.0 2.9 fusion.168
  551.9 4.3 fusion.167
  556.2 3.8 collective-permute-done.1
  568.5 2.9 fusion.168
  571.4 4.3 fusion.167
  575.7 3.8 collective-permute-done.1
  588.1 2.9 fusion.168
  591.0 4.3 fusion.167
  595.2 3.8 collective-permute-done.1
  607.6 2.9 fusion.168
  610.5 4.3 fusion.167
  614.8 3.8 collective-permute-done.1
  627.1 2.9 fusion.168
  630.0 4.3 fusion.167
  634.3 3.8 collective-permute-done.1
  638.1 2.1 fusion.56
  640.2 2.0 copy.19
  642.3 5.2 copy.18
  649.6 5.0 fusion.53
  654.6 323.6 %reduce-scatter.7.cloned.1.call-done = f32[64,64]{1,0:T(8,128)} async-done(((f32[4096,64]{1,0:T(8,128)}), f32[64,64]{1,0:T(8,128)}) %reduce-scatter.7.cloned.1.call-update) | async-done | bytes 16400
  979.7 323.7 %reduce-scatter.5.cloned.1.call-done = f32[64,192]{1,0:T(8,128)} async-done(((f32[4096,192]{1,0:T(8,128)}), f32[64,192]{1,0:T(8,128)}) %reduce-scatter.5.cloned.1.call-update) | async-done | bytes 49168 | tf_op jit(solution)/shard_map/reduce_scatter | solution.py:108
  (398 shorter events, 128.2 us)
Async XLA Ops:
  7.2 191.2 %copy-start.9 = (bf16[1,4096]{1,0:T(2,128)(2,1)S(1)}, bf16[1,4096]{1,0:T(2,128)(2,1)}, u32[]{:S(2)}) copy-start(bf16[1,4096]{1,0:T(2,128)(2,1)} %param.13) | copy-start | bytes 24580
  7.2 312.2 %all-gather.4.cloned.1.call-start = ((), (), s32[]{:S(2)}) async-start(), calls=%async_computation.3 | async-start | bytes 2129920 | tf_op jit(solution)/shard_map/all_gather | solution.py:47
  7.9 970.3 %reduce-scatter.7.cloned.1.call-start = ((), (), s32[]{:S(2)}) async-start(), calls=%async_computation.4 | async-start | bytes 2129920
  320.3 3.9 copy-start
  326.7 11.5 collective-permute-start
  339.0 3.9 copy-start
  345.4 11.5 collective-permute-start
  357.6 3.9 copy-start
  364.1 13.6 %collective-permute-start = (bf16[64,4096]{1,0:T(8,128)(2,1)S(1)}, bf16[64,4096]{1,0:T(8,128)(2,1)S(1)}, u32[]{:S(2)}, u32[]{:S(2)}) collective-permute-start(bf16[64,4096]{1,0:T(8,128)(2,1)S(1)} %fusion.145), channel_id=1, source_target_pairs={{0,64},{64,128},{128,192},{192,256},{256,320},{320,384},{384,448},... | collective-permute-start | bytes 1572872 | tf_op jit(solution)/shard_map/while/body/eval_jaxpr/ppermute | solution.py:10
  378.4 3.9 copy-start
  384.8 12.7 collective-permute-start
  398.3 3.9 copy-start
  404.7 12.7 collective-permute-start
  418.2 3.9 copy-start
  424.6 12.6 collective-permute-start
  438.0 3.9 copy-start
  444.4 12.6 collective-permute-start
  457.8 3.9 copy-start
  464.2 12.7 collective-permute-start
  477.6 1.9 copy-start.1
  482.4 1.2 copy-start.7
  482.4 2.3 copy-start.4
  484.7 3.0 copy-start.2
  487.8 12.9 collective-permute-start.1
  501.9 2.3 copy-start.4
  504.2 3.0 copy-start.2
  507.3 13.7 %collective-permute-start.1 = (bf16[64,4096]{1,0:T(8,128)(2,1)}, bf16[64,4096]{1,0:T(8,128)(2,1)}, u32[]{:S(2)}, u32[]{:S(2)}) collective-permute-start(bf16[64,4096]{1,0:T(8,128)(2,1)} %fusion.166), channel_id=1, source_target_pairs={{64,0},{128,64},{192,128},{256,192},{320,256},{384,320},{448,384},... | collective-permute-start | bytes 1572872 | tf_op jit(solution)/shard_map/while/body/eval_jaxpr/ppermute | solution.py:10
  522.2 2.3 copy-start.4
  524.5 3.0 copy-start.2
  527.6 12.9 collective-permute-start.1
  541.7 2.3 copy-start.4
  544.0 3.0 copy-start.2
  547.1 12.9 collective-permute-start.1
  561.3 2.3 copy-start.4
  563.6 3.0 copy-start.2
  566.6 12.9 collective-permute-start.1
  580.8 2.3 copy-start.4
  583.1 3.0 copy-start.2
  586.1 12.9 collective-permute-start.1
  600.3 2.3 copy-start.4
  602.6 3.0 copy-start.2
  605.7 12.9 collective-permute-start.1
  619.8 2.3 copy-start.4
  622.2 3.0 copy-start.2
  625.2 12.9 collective-permute-start.1
  642.2 661.2 %reduce-scatter.5.cloned.1.call-start = ((), (), s32[]{:S(2)}) async-start(), calls=%async_computation.2 | async-start | bytes 4259840 | tf_op jit(solution)/shard_map/reduce_scatter | solution.py:108
  642.2 5.3 copy-start.5
  642.3 5.3 copy-start.8
  (23 other events, 21.2 us)
Sparse Core Ops, SparseCore 0:
  10.1 309.1 all-gather.3
  642.3 335.8 reduce-scatter.6
  981.8 321.5 reduce-scatter.4
where the time goes:
time: 1310 us
  waiting for transfers between devices  831 us (63%)
  blocking collectives  185 us (14%)
  matrix products  104 us (8%)
  starting transfers between devices  87 us (7%)
  local copies, waits for them, and re-layouts  39.2 us (3%)
  other arithmetic  38.6 us (3%)
  between operations  13.9 us (1%)
    unnamed x4, waiting for transfers between devices  324 us
    reduce_scatter x1, waiting for transfers between devices, body(): lax.psum_scatter(sum_qkv, 'dp', scatter_dimension=0, tiled=True)  324 us
    all_gather x1, blocking collectives, body(): lax.all_gather(w_out[0], 'dp', axis=1, tiled=True)  185 us
    all_gather x1, waiting for transfers between devices, body(): lax.all_gather(w_qkv[0], 'dp', axis=0, tiled=True)  121 us
    ppermute x16, starting transfers between devices, passed_along(): return lax.ppermute(block, axis, route)  86.9 us
    ppermute x16, waiting for transfers between devices, passed_along(): return lax.ppermute(block, axis, route)  61.8 us
    dot_general x34, matrix products, layer(): jnp.dot(normed, w_qkv, preferred_element_type=jnp.float32)  52.9 us
    dot_general x26, matrix products, layer(): jnp.dot(attended, w_out, preferred_element_type=jnp.float32)  41.8 us
  transfers between devices with their start and end apart: 19, of which 19 were waited for; matrix products, arithmetic and copies ran while one was open for 6% of the time, Pallas kernels for 0%

commit v1 on v0

--- a/solution.py
+++ b/solution.py
@@ -2,6 +2,11 @@
 import jax.numpy as jnp
 from jax import lax
 from jax.sharding import PartitionSpec as P
+
+
+def swapped_in(x, name, dim):
+    sent = jnp.stack([x] * lax.axis_size(name))
+    return jnp.concatenate(lax.all_to_all(sent, name, 0, 0), axis=dim)
 
 
 def passed_along(block, axis, distance):
@@ -45,7 +50,7 @@
     gain = norm_gain[0]
     full_qkv, full_out = (
         lax.all_gather(w_qkv[0], "dp", axis=0, tiled=True),
-        lax.all_gather(w_out[0], "dp", axis=1, tiled=True),
+        swapped_in(w_out[0], "dp", 1),
     )
     total_steps = micro + sections - 1
     empty = jnp.zeros(inputs.shape[1:], inputs.dtype)

time: 1310 us -> 1310 us (level)
  waiting for transfers between devices: 831 us -> 814 us
  starting transfers between devices: 87 us -> 102 us
    all_to_all x0 -> x1, starting transfers between devices: none -> 14.9 us  [swapped_in(): return jnp.concatenate(lax.all_to_all(sent, name, 0, 0), axis=dim)]
  transfers between devices with their start and end apart: 19 -> 20, of which waited for: 19 -> 19; matrix products, arithmetic and copies ran while one was open for 6% -> 6% of each run, Pallas kernels for 0% -> 0%
where the time goes in v1:
time: 1310 us
  waiting for transfers between devices  814 us (62%)
  blocking collectives  179 us (14%)
  matrix products  104 us (8%)
  starting transfers between devices  102 us (8%)
  local copies, waits for them, and re-layouts  44.2 us (3%)
  other arithmetic  38 us (3%)
  between operations  14 us (1%)
    reduce_scatter x1, waiting for transfers between devices, body(): lax.psum_scatter(sum_qkv, 'dp', scatter_dimension=0, tiled=True)  323 us
    unnamed x4, waiting for transfers between devices  321 us
    all_gather x1, blocking collectives, body(): lax.all_gather(w_out[0], 'dp', axis=1, tiled=True)  179 us
    all_gather x1, waiting for transfers between devices, body(): lax.all_gather(w_qkv[0], 'dp', axis=0, tiled=True)  108 us
    ppermute x16, starting transfers between devices, passed_along(): return lax.ppermute(block, axis, route)  86.6 us
    ppermute x16, waiting for transfers between devices, passed_along(): return lax.ppermute(block, axis, route)  61.8 us
    dot_general x34, matrix products, layer(): jnp.dot(normed, w_qkv, preferred_element_type=jnp.float32)  52.9 us
    dot_general x26, matrix products, layer(): jnp.dot(attended, w_out, preferred_element_type=jnp.float32)  41.8 us
  transfers between devices with their start and end apart: 20, of which 19 were waited for; matrix products, arithmetic and copies ran while one was open for 6% of the time, Pallas kernels for 0%

profile of v1, /device:TPU:16, one launch (start us, length us, event | category | flops | bytes accessed | tf_op | source)
XLA Modules:
  0.0 1306.6 jit_solution(3197488363103180503)
XLA Ops:
  10.4 14.9 %all-to-all-start = ((bf16[64,2,2048]{2,1,0:T(2,128)(2,1)}), bf16[64,2,2048]{2,1,0:T(2,128)(2,1)S(1)}, u32[]{:S(2)}, u32[]{:S(2)}) async-start(bf16[64,2,2048]{2,1,0:T(2,128)(2,1)} %reshape.103), calls=%async_computation | async-start | bytes 1048576 | tf_op jit(solution)/shard_map/all_to_all | solution.py:9
  25.8 179.0 %all-gather.1 = bf16[1,64,4096]{1,0,2:T(2,128)(2,1)S(1)} all-gather(bf16[1,64,64]{1,0,2:T(2,128)(2,1)S(1)} %copy.17), channel_id=3, replica_groups=mesh['section'=8,'dp'=64] {'dp'}, dimensions={2}, use_global_device_ids=true | all-gather | bytes 532480 | tf_op jit(solution)/shard_map/all_gather | solution.py:83
  204.7 3.6 copy.18
  211.5 108.2 %all-gather.4.cloned.1.call-done = bf16[1,4096,192]{2,1,0:T(8,128)(2,1)} async-done(((bf16[1,64,192]{2,1,0:T(8,128)(2,1)}), bf16[1,4096,192]{2,1,0:T(8,128)(2,1)}) %all-gather.4.cloned.1.call-update) | async-done | bytes 1572880 | tf_op jit(solution)/shard_map/all_gather | solution.py:52
  320.7 157.3 %while.30 = (s32[]{:T(128)}, bf16[64,4096]{1,0:T(8,128)(2,1)}, bf16[2,64,4096]{2,1,0:T(8,128)(2,1)S(1)}, pred[]{:T(512)}, s32[8]{0:T(128)S(1)}, /*index=5*/s32[]...) while((s32[]{:T(128)}, bf16[64,4096]{1,0:T(8,128)(2,1)}, ...), condition=%wide.region_6.7_spmd, body=%wide.region_2.6_spmd.sunk | while | flops 138477504 | bytes 20632148 | solution.py:77
  327.1 1.9 collective-permute-start
  329.1 9.6 collective-permute-done
  345.8 1.9 collective-permute-start
  347.8 9.6 collective-permute-done
  364.5 11.8 collective-permute-start
  385.1 11.2 collective-permute-start
  405.0 11.1 collective-permute-start
  424.9 11.1 collective-permute-start
  444.7 11.1 collective-permute-start
  464.5 11.1 collective-permute-start
  481.5 157.0 %while.31 = (s32[]{:T(128)}, bf16[64,4096]{1,0:T(8,128)(2,1)}, f32[4096,192]{0,1:T(8,128)}, f32[64,4096]{1,0:T(8,128)}, pred[]{:T(512)}, /*index=5*/s32[8]{0:T(1...) while((s32[]{:T(128)}, bf16[64,4096]{1,0:T(8,128)(2,1)}, ...), condition=%wide.region_13.14_spmd.clone, body=%wide.region_7.13_spmd.clone.sunk | while | flops 384602496 | bytes 32000636 | solution.py:108
  488.1 1.9 collective-permute-start.1
  490.0 2.6 fusion.168
  492.6 2.4 fusion.167
  495.0 6.0 collective-permute-done.1
  507.6 1.9 collective-permute-start.1
  509.5 2.9 fusion.168
  512.4 4.3 fusion.167
  516.7 4.6 collective-permute-done.1
  529.8 2.9 fusion.168
  532.7 4.3 fusion.167
  537.0 3.8 collective-permute-done.1
  549.3 2.9 fusion.168
  552.2 4.3 fusion.167
  556.5 3.8 collective-permute-done.1
  568.9 2.9 fusion.168
  571.8 4.3 fusion.167
  576.0 3.8 collective-permute-done.1
  588.4 2.9 fusion.168
  591.3 4.3 fusion.167
  595.6 3.8 collective-permute-done.1
  607.9 2.9 fusion.168
  610.8 4.3 fusion.167
  615.1 3.8 collective-permute-done.1
  627.5 2.9 fusion.168
  630.4 4.3 fusion.167
  634.6 3.8 collective-permute-done.1
  638.4 2.1 fusion.56
  640.5 2.0 copy.20
  642.6 5.2 copy.19
  649.9 5.0 fusion.53
  654.9 320.3 %reduce-scatter.7.cloned.1.call-done = f32[64,64]{1,0:T(8,128)} async-done(((f32[4096,64]{1,0:T(8,128)}), f32[64,64]{1,0:T(8,128)}) %reduce-scatter.7.cloned.1.call-update) | async-done | bytes 16400
  976.6 323.4 %reduce-scatter.5.cloned.1.call-done = f32[64,192]{1,0:T(8,128)} async-done(((f32[4096,192]{1,0:T(8,128)}), f32[64,192]{1,0:T(8,128)}) %reduce-scatter.5.cloned.1.call-update) | async-done | bytes 49168 | tf_op jit(solution)/shard_map/reduce_scatter | solution.py:113
  (409 shorter events, 134.4 us)
Async XLA Ops:
  7.2 18.3 %copy-start.9 = (bf16[1,64,64]{2,1,0:T(8,128)(2,1)S(1)}, bf16[1,64,64]{2,1,0:T(8,128)(2,1)}, u32[]{:S(2)}) copy-start(bf16[1,64,64]{2,1,0:T(8,128)(2,1)} %param.15) | copy-start | bytes 24580
  7.2 18.4 %copy-start.11 = (s32[2,1,2]{2,1,0:T(1,128)S(1)}, s32[2,1,2]{2,1,0:T(1,128)}, u32[]{:S(2)}) copy-start(s32[2,1,2]{2,1,0:T(1,128)} %param.12) | copy-start | bytes 52
  7.2 312.6 %all-gather.4.cloned.1.call-start = ((), (), s32[]{:S(2)}) async-start(), calls=%async_computation.4 | async-start | bytes 2129920 | tf_op jit(solution)/shard_map/all_gather | solution.py:52
  10.4 197.9 %copy-start.10 = (bf16[1,4096]{1,0:T(2,128)(2,1)S(1)}, bf16[1,4096]{1,0:T(2,128)(2,1)}, u32[]{:S(2)}) copy-start(bf16[1,4096]{1,0:T(2,128)(2,1)} %param.13) | copy-start | bytes 24580
  10.4 198.1 %all-to-all-start = ((bf16[64,2,2048]{2,1,0:T(2,128)(2,1)}), bf16[64,2,2048]{2,1,0:T(2,128)(2,1)S(1)}, u32[]{:S(2)}, u32[]{:S(2)}) async-start(bf16[64,2,2048]{2,1,0:T(2,128)(2,1)} %reshape.103), calls=%async_computation | async-start | bytes 1048576 | tf_op jit(solution)/shard_map/all_to_all | solution.py:9
  25.4 949.8 %reduce-scatter.7.cloned.1.call-start = ((), (), s32[]{:S(2)}) async-start(), calls=%async_computation.5 | async-start | bytes 2129920
  320.7 3.9 copy-start
  327.1 11.5 collective-permute-start
  339.4 3.9 copy-start
  345.8 11.5 collective-permute-start
  358.1 3.9 copy-start
  364.5 13.3 %collective-permute-start = (bf16[64,4096]{1,0:T(8,128)(2,1)S(1)}, bf16[64,4096]{1,0:T(8,128)(2,1)S(1)}, u32[]{:S(2)}, u32[]{:S(2)}) collective-permute-start(bf16[64,4096]{1,0:T(8,128)(2,1)S(1)} %fusion.145), channel_id=1, source_target_pairs={{0,64},{64,128},{128,192},{192,256},{256,320},{320,384},{384,448},... | collective-permute-start | bytes 1572872 | tf_op jit(solution)/shard_map/while/body/eval_jaxpr/ppermute | solution.py:15
  378.7 3.9 copy-start
  385.1 12.7 collective-permute-start
  398.6 3.9 copy-start
  405.0 12.7 collective-permute-start
  418.5 3.9 copy-start
  424.9 12.6 collective-permute-start
  438.3 3.9 copy-start
  444.7 12.6 collective-permute-start
  458.1 3.9 copy-start
  464.5 12.7 collective-permute-start
  485.1 3.0 copy-start.2
  488.1 12.9 collective-permute-start.1
  502.3 2.3 copy-start.5
  504.6 3.0 copy-start.2
  507.6 13.7 %collective-permute-start.1 = (bf16[64,4096]{1,0:T(8,128)(2,1)}, bf16[64,4096]{1,0:T(8,128)(2,1)}, u32[]{:S(2)}, u32[]{:S(2)}) collective-permute-start(bf16[64,4096]{1,0:T(8,128)(2,1)} %fusion.166), channel_id=1, source_target_pairs={{64,0},{128,64},{192,128},{256,192},{320,256},{384,320},{448,384},... | collective-permute-start | bytes 1572872 | tf_op jit(solution)/shard_map/while/body/eval_jaxpr/ppermute | solution.py:15
  522.5 2.3 copy-start.5
  524.8 3.0 copy-start.2
  527.9 12.9 collective-permute-start.1
  542.1 2.3 copy-start.5
  544.4 3.0 copy-start.2
  547.4 12.9 collective-permute-start.1
  561.6 2.3 copy-start.5
  563.9 3.0 copy-start.2
  566.9 12.9 collective-permute-start.1
  581.1 2.3 copy-start.5
  583.4 3.0 copy-start.2
  586.5 12.9 collective-permute-start.1
  600.6 2.3 copy-start.5
  603.0 3.0 copy-start.2
  606.0 12.9 collective-permute-start.1
  620.2 2.3 copy-start.5
  622.5 3.0 copy-start.2
  625.5 12.9 collective-permute-start.1
  642.5 657.5 %reduce-scatter.5.cloned.1.call-start = ((), (), s32[]{:S(2)}) async-start(), calls=%async_computation.3 | async-start | bytes 4259840 | tf_op jit(solution)/shard_map/reduce_scatter | solution.py:113
  642.6 5.3 copy-start.6
  642.6 5.3 copy-start.8
  (26 other events, 27.1 us)
Sparse Core Ops, SparseCore 0:
  10.1 309.6 all-gather.3
  642.6 332.4 reduce-scatter.6
  978.8 321.2 reduce-scatter.4
